TPU v7x, 256 devices: a whole 4x4x8 slice. The times are simulated.
256 devices in a mesh: con: 16 (over z_hi, x, core), res: 16 (over y, z_lo).
Axes of the slice: x: 4, y: 4, z: 8 (z_hi: 2, z_lo: 4; z = z_hi * 4 + z_lo), core: 2. Of those that a mesh axis runs over, the one named last changes fastest.
Arguments:
- integrals: float32 [24576, 24576], P('res', 'con'), as said below
- tile_mask: int32 [96, 96], P('res', 'con'), may hold values from 0 to 1, as said below
- amplitudes: float32 [24576, 384], P(('con', 'res')), may hold values from -4 to 4
- other_first: float32 [24576, 384], P(('res', 'con')), may hold values from -6 to 6
- other_second: float32 [24576, 384], P(('con', 'res')), may hold values from -6 to 6
- vir_index: int32 [2, 24576], replicated, may hold values from 0 to 1599
- occ_index: int32 [2, 384], replicated, may hold values from 0 to 31, as said below
- partner: int32 [384], replicated, may hold values from 0 to 383, as said below
- eps_vir: float32 [1600], replicated, may hold values from 0.2 to 3
- eps_occ: float32 [32], replicated, may hold values from -2 to -0.2
Outputs:
- first_update: float32 [24576, 384], P(('res', 'con'))
- second_update: float32 [24576, 384], P(('con', 'res'))
Inputs may be any that keep to these rules, and one draw needn't show every extreme that they name: integrals is symmetric: integrals[p, s] == integrals[s, p]. tile_mask is symmetric and its diagonal is 1. partner is a permutation that is its own inverse with no fixed point. The two orbitals of an occupied pair differ, and occ_index[0, partner[q]] == occ_index[1, q].
All inputs are finite; a program needn't handle non-finite values.
Results may differ from a plain program's by a relative error of at most 0.000065.
Values sent between devices are 32-bit elements; how exact they have to be, the bound alone decides.
A program may use at most 128 MiB of HBM per device.

v0:
```python
import jax
import jax.numpy as jnp
from jax import lax
from jax.sharding import PartitionSpec as P

W = 256
exact = lax.Precision.HIGHEST
three = lax.Precision.HIGH


def pick(index, table):
    places = lax.broadcasted_iota(jnp.int32, (index.shape[0], table.shape[0]), 1)
    hits = (index[:, None] == places).astype(jnp.float32)
    return jnp.sum(hits * table[None, :], axis=1)


def pair_energy(pair_index, table):
    return pick(pair_index[0], table) + pick(pair_index[1], table)


def pair_map(partner):
    cols = partner.shape[0]
    here = lax.broadcasted_iota(jnp.int32, (cols,), 0)
    first = here < partner
    key = jnp.minimum(here, partner)
    couple = jnp.sum((first[None, :] & (here[None, :] < key[:, None])).astype(jnp.int32), axis=1)
    hit = couple[:, None] == lax.broadcasted_iota(jnp.int32, (cols, cols // 2), 1)
    return jnp.where(hit, jnp.where(first, 1.0, -1.0)[:, None], 0.0)


def per_device(
    integrals,
    tile_mask,
    amplitudes,
    other_first,
    other_second,
    vir_index,
    occ_index,
    partner,
    eps_vir,
    eps_occ,
):
    row_count, col_count = integrals.shape
    tiles_down, tiles_across = tile_mask.shape
    weights = tile_mask.astype(jnp.float32)
    screened = (
        integrals.reshape(tiles_down, W, tiles_across, W) * weights[:, None, :, None]
    ).reshape(row_count, col_count)
    pairs = pair_map(partner)
    occ_energy = pair_energy(occ_index, eps_occ)
    occ_energy = jnp.sum(jnp.where(pairs > 0, occ_energy[:, None], 0.0), axis=0)
    n_con = lax.axis_size("con")
    n_res = lax.axis_size("res")
    con_at = lax.axis_index("con")
    res_at = lax.axis_index("res")
    fine_rows = amplitudes.shape[0]

    def differences(block):
        return jnp.dot(block, pairs, precision=exact, preferred_element_type=jnp.float32)

    def spread(half):
        return 0.5 * lax.dot_general(
            half,
            pairs,
            (((1,), (1,)), ((), ())),
            precision=exact,
            preferred_element_type=jnp.float32,
        )

    def denominator(offset):
        picked = lax.dynamic_slice_in_dim(vir_index, offset, fine_rows, 1)
        return pair_energy(picked, eps_vir)[:, None] - occ_energy[None, :]

    own = differences(amplitudes)
    partial_one = jnp.dot(
        screened,
        lax.all_gather(own, "res", axis=0, tiled=True),
        precision=three,
        preferred_element_type=jnp.float32,
    )
    ladder_one = lax.psum_scatter(partial_one, "con", scatter_dimension=0, tiled=True)
    first = (differences(other_first) + ladder_one) / denominator(
        (res_at * n_con + con_at) * fine_rows
    )
    partial_two = lax.dot_general(
        screened,
        lax.all_gather(first, "con", axis=0, tiled=True),
        (((0,), (0,)), ((), ())),
        precision=three,
        preferred_element_type=jnp.float32,
    )
    ladder_two = lax.psum_scatter(partial_two, "res", scatter_dimension=0, tiled=True)
    second = (differences(other_second) + ladder_two) / denominator(
        (con_at * n_res + res_at) * fine_rows
    )
    return (spread(first), spread(second))


def solution(mesh):
    return jax.shard_map(
        per_device,
        mesh=mesh,
        in_specs=(
            P("res", "con"),
            P("res", "con"),
            P(("con", "res"), None),
            P(("res", "con"), None),
            P(("con", "res"), None),
            P(),
            P(),
            P(),
            P(),
            P(),
        ),
        out_specs=(P(("res", "con"), None), P(("con", "res"), None)),
        check_vma=False,
    )
```

profile of v0, /device:TPU:4, one launch (start us, length us, event | category | flops | bytes accessed | tf_op | source)
XLA Modules:
  0.0 355.9 jit_solution(8949137891145068009)
XLA Ops:
  7.2 0.7 broadcast_select_fusion
  7.9 0.7 iota_minimum_fusion
  8.9 0.4 convolution_bitcast_fusion.1
  9.3 0.7 copy.18
  10.1 0.7 convert_element_type.5
  10.8 0.9 mul.69
  11.7 8.4 %copy.28 = f32[192,8,6,256]{3,1,2,0:T(8,128)} copy(f32[192,8,6,256]{3,2,1,0:T(8,128)S(1)} %bitcast.36) | data formatting | bytes 18874368
  20.0 12.2 %mul.71 = f32[1536,1536]{1,0:T(8,128)} multiply(f32[1536,1536]{1,0:T(8,128)} %param.10, f32[1536,1536]{1,0:T(8,128)} %bitcast.37) | non-fusion elementwise | flops 2359296 | bytes 28311552 | tf_op jit(solution)/shard_map/mul | solution.py:47
  32.3 65.8 %all-gather.3.cloned.1.call-done = f32[1536,192]{1,0:T(8,128)} async-done(((f32[96,192]{1,0:T(8,128)}), f32[1536,192]{1,0:T(8,128)}) %all-gather.3.cloned.1.call-update) | async-done | bytes 1179664 | tf_op jit(solution)/shard_map/all_gather | solution.py:77
  98.1 9.3 %fusion.30 = f32[1536,192]{1,0:T(8,128)} fusion(f32[1536,1536]{1,0:T(8,128)} %mul.71, f32[1536,192]{1,0:T(8,128)} %all-gather.3.cloned.1.call-done), kind=kOutput, calls=%fused_computation.63 | convolution fusion | flops 2717908992 | bytes 11796480
  107.5 0.6 copy-done.2
  108.2 0.8 constant_dynamic-slice_fusion.1
  109.0 0.5 select_reduce_fusion
  109.6 78.8 %reduce-scatter.7.cloned.1.call-done = f32[96,192]{1,0:T(8,128)} async-done(((f32[1536,192]{1,0:T(8,128)}), f32[96,192]{1,0:T(8,128)}) %reduce-scatter.7.cloned.1.call-update) | async-done | bytes 73744
  188.4 1.0 copy.25
  189.4 0.4 fusion.3
  189.9 0.7 copy.20
  190.7 56.7 %all-gather.5.cloned.1.call-done = f32[1536,192]{1,0:T(8,128)} async-done(((f32[96,192]{1,0:T(8,128)}), f32[1536,192]{1,0:T(8,128)}) %all-gather.5.cloned.1.call-update) | async-done | bytes 1179664 | tf_op jit(solution)/shard_map/all_gather | solution.py:87
  247.4 12.8 %fusion.31 = f32[1536,192]{1,0:T(8,128)} fusion(f32[1536,1536]{1,0:T(8,128)} %mul.71, f32[1536,192]{1,0:T(8,128)} %all-gather.5.cloned.1.call-done), kind=kOutput, calls=%fused_computation.64 | convolution fusion | flops 2717908992 | bytes 11796480
  260.2 1.1 convolution_multiply_fusion.1
  261.3 85.5 %reduce-scatter.9.cloned.1.call-done = f32[96,192]{1,0:T(8,128)} async-done(((f32[1536,192]{1,0:T(8,128)}), f32[96,192]{1,0:T(8,128)}) %reduce-scatter.9.cloned.1.call-update) | async-done | bytes 73744
  346.8 1.0 copy.27
  347.8 0.4 fusion.1
  348.3 1.1 convolution_multiply_fusion
  (27 shorter events, 0.8 us)
Async XLA Ops:
  7.2 1.7 copy-start
  7.2 90.9 %all-gather.3.cloned.1.call-start = ((), (), s32[]{:S(2)}) async-start(), calls=%async_computation.2 | async-start | bytes 1671168 | tf_op jit(solution)/shard_map/all_gather | solution.py:77
  10.0 178.4 %reduce-scatter.7.cloned.1.call-start = ((), (), s32[]{:S(2)}) async-start(), calls=%async_computation.4 | async-start | bytes 1671168
  107.4 0.7 copy-start.2
  107.4 0.7 copy-start.3
  107.4 1.6 copy-start.1
  107.4 82.0 %copy-start.4 = (f32[96,384]{1,0:T(8,128)S(1)}, f32[96,384]{1,0:T(8,128)}, u32[]{:S(2)}) copy-start(f32[96,384]{1,0:T(8,128)} %param.13) | copy-start | bytes 442372
  107.4 139.9 %all-gather.5.cloned.1.call-start = ((), (), s32[]{:S(2)}) async-start(), calls=%async_computation.3 | async-start | bytes 1671168 | tf_op jit(solution)/shard_map/all_gather | solution.py:87
  190.6 156.2 %reduce-scatter.9.cloned.1.call-start = ((), (), s32[]{:S(2)}) async-start(), calls=%async_computation.5 | async-start | bytes 1671168
  260.2 87.6 %copy-start.5 = (f32[96,384]{1,0:T(8,128)S(1)}, f32[96,384]{1,0:T(8,128)}, u32[]{:S(2)}) copy-start(f32[96,384]{1,0:T(8,128)} %param.14) | copy-start | bytes 442372
Sparse Core Ops, SparseCore 0:
  10.4 87.6 all-gather.2
  107.5 80.8 reduce-scatter.6
  191.8 55.5 all-gather.4
  260.4 86.4 reduce-scatter.8
where the time goes:
time: 356 us
  waiting for transfers between devices  287 us (81%)
  matrix products  25.5 us (7%)
  other arithmetic  15.3 us (4%)
  local copies, waits for them, and re-layouts  14.1 us (4%)
  between operations  13.9 us (4%)
    unnamed x6, waiting for transfers between devices  164 us
    all_gather x1, waiting for transfers between devices, per_device(): lax.all_gather(own, 'res', axis=0, tiled=True)  65.8 us
    all_gather x1, waiting for transfers between devices, per_device(): lax.all_gather(first, 'con', axis=0, tiled=True)  56.7 us
    unnamed x2, matrix products  22.1 us
    mul x1, other arithmetic, per_device(): integrals.reshape(tiles_down, W, tiles_across, W)  12.2 us
    unnamed x15, local copies, waits for them, and re-layouts  10.9 us
  transfers between devices with their start and end apart: 4, of which 4 were waited for; matrix products, arithmetic and copies ran while one was open for 7% of the time, Pallas kernels for 0%

commit v1 on v0

--- a/solution.py
+++ b/solution.py
@@ -6,6 +6,13 @@
 W = 256
 exact = lax.Precision.HIGHEST
 three = lax.Precision.HIGH
+
+
+def exchange_gather(x, mesh_axis, d):
+    n_dev = lax.axis_size(mesh_axis)
+    tiles = jnp.stack([x for _ in range(n_dev)])
+    tiles = lax.all_to_all(tiles, mesh_axis, split_axis=0, concat_axis=0)
+    return jnp.concatenate(tiles, axis=d)
 
 
 def pick(index, table):
@@ -84,7 +91,7 @@
     )
     partial_two = lax.dot_general(
         screened,
-        lax.all_gather(first, "con", axis=0, tiled=True),
+        exchange_gather(first, "con", 0),
         (((0,), (0,)), ((), ())),
         precision=three,
         preferred_element_type=jnp.float32,

time: 356 us -> 344 us (0.966)
  waiting for transfers between devices: 287 us -> 247 us
  blocking collectives: 0 us -> 29.7 us
    all_gather x1 -> x0, waiting for transfers between devices: 56.7 us -> none  [per_device(): lax.all_gather(first, 'con', axis=0, tiled=True)]
    all_to_all x0 -> x1, blocking collectives: none -> 29.7 us  [exchange_gather(): tiles = lax.all_to_all(tiles, mesh_axis, split_axis=0, concat_axis=0)]
    unnamed x6 -> x5, waiting for transfers between devices: 164 us -> 181 us
  transfers between devices with their start and end apart: 4 -> 3, of which waited for: 4 -> 3; matrix products, arithmetic and copies ran while one was open for 7% -> 7% of each run, Pallas kernels for 0% -> 0%
where the time goes in v1:
time: 344 us
  waiting for transfers between devices  247 us (72%)
  blocking collectives  29.7 us (9%)
  matrix products  24 us (7%)
  other arithmetic  15.3 us (4%)
  between operations  13.9 us (4%)
  local copies, waits for them, and re-layouts  13.6 us (4%)
    unnamed x5, waiting for transfers between devices  181 us
    all_gather x1, waiting for transfers between devices, per_device(): lax.all_gather(own, 'res', axis=0, tiled=True)  65.8 us
    all_to_all x1, blocking collectives, exchange_gather(): tiles = lax.all_to_all(tiles, mesh_axis, split_axis=0, concat_axis=0)  29.7 us
    unnamed x2, matrix products  20.7 us
    mul x1, other arithmetic, per_device(): integrals.reshape(tiles_down, W, tiles_across, W)  12.2 us
    unnamed x15, local copies, waits for them, and re-layouts  10.9 us
  transfers between devices with their start and end apart: 3, of which 3 were waited for; matrix products, arithmetic and copies ran while one was open for 7% of the time, Pallas kernels for 0%

profile of v1, /device:TPU:4, one launch (start us, length us, event | category | flops | bytes accessed | tf_op | source)
XLA Modules:
  0.0 343.6 jit_solution(12973362117167730066)
XLA Ops:
  7.2 0.7 broadcast_select_fusion
  7.9 0.7 iota_minimum_fusion
  8.6 0.2 convert_reduce_fusion
  8.9 0.4 convolution_bitcast_fusion.1
  9.3 0.7 copy.20
  10.1 0.7 convert_element_type.5
  10.8 0.9 mul.69
  11.7 8.4 %copy.30 = f32[192,8,6,256]{3,1,2,0:T(8,128)} copy(f32[192,8,6,256]{3,2,1,0:T(8,128)S(1)} %bitcast.37) | data formatting | bytes 18874368
  20.0 12.2 %mul.71 = f32[1536,1536]{1,0:T(8,128)} multiply(f32[1536,1536]{1,0:T(8,128)} %param.10, f32[1536,1536]{1,0:T(8,128)} %bitcast.38) | non-fusion elementwise | flops 2359296 | bytes 28311552 | tf_op jit(solution)/shard_map/mul | solution.py:54
  32.3 65.8 %all-gather.2.cloned.1.call-done = f32[1536,192]{1,0:T(8,128)} async-done(((f32[96,192]{1,0:T(8,128)}), f32[1536,192]{1,0:T(8,128)}) %all-gather.2.cloned.1.call-update) | async-done | bytes 1179664 | tf_op jit(solution)/shard_map/all_gather | solution.py:84
  98.1 9.3 %fusion.30 = f32[1536,192]{1,0:T(8,128)} fusion(f32[1536,1536]{1,0:T(8,128)} %mul.71, f32[1536,192]{1,0:T(8,128)} %all-gather.2.cloned.1.call-done), kind=kOutput, calls=%fused_computation.63 | convolution fusion | flops 2717908992 | bytes 11796480
  107.5 0.6 copy-done.2
  108.2 0.8 constant_dynamic-slice_fusion.1
  109.0 0.5 select_reduce_fusion
  109.6 78.8 %reduce-scatter.7.cloned.1.call-done = f32[96,192]{1,0:T(8,128)} async-done(((f32[1536,192]{1,0:T(8,128)}), f32[96,192]{1,0:T(8,128)}) %reduce-scatter.7.cloned.1.call-update) | async-done | bytes 73744
  188.4 1.0 copy.27
  189.4 0.4 fusion.3
  190.1 29.7 %all_to_all.5 = f32[16,96,192]{2,1,0:T(8,128)S(1)} all-to-all(f32[16,96,192]{2,1,0:T(8,128)S(1)} %stack.2), channel_id=1, replica_groups=mesh['con'=16,'res'=16] {'con'}, dimensions={0} | all-to-all | bytes 2359296 | tf_op jit(solution)/shard_map/all_to_all | solution.py:14
  219.8 11.3 %fusion.31 = f32[1536,192]{1,0:T(8,128)} fusion(f32[1536,1536]{1,0:T(8,128)} %mul.71, f32[1536,192]{1,0:T(8,128)S(1)} %bitcast.39), kind=kOutput, calls=%fused_computation.64 | convolution fusion | flops 2717908992 | bytes 11796480
  231.2 1.1 convolution_multiply_fusion.1
  232.2 102.3 %reduce-scatter.9.cloned.1.call-done = f32[96,192]{1,0:T(8,128)} async-done(((f32[1536,192]{1,0:T(8,128)}), f32[96,192]{1,0:T(8,128)}) %reduce-scatter.9.cloned.1.call-update) | async-done | bytes 73744
  334.6 1.0 copy.29
  335.6 0.4 fusion.1
  336.0 1.1 convolution_multiply_fusion
  (26 shorter events, 0.7 us)
Async XLA Ops:
  7.2 1.7 copy-start
  7.2 90.9 %all-gather.2.cloned.1.call-start = ((), (), s32[]{:S(2)}) async-start(), calls=%async_computation.3 | async-start | bytes 1671168 | tf_op jit(solution)/shard_map/all_gather | solution.py:84
  10.0 178.4 %reduce-scatter.7.cloned.1.call-start = ((), (), s32[]{:S(2)}) async-start(), calls=%async_computation.4 | async-start | bytes 1671168
  107.4 0.7 copy-start.2
  107.4 0.7 copy-start.3
  107.4 1.6 copy-start.1
  107.4 82.0 %copy-start.4 = (f32[96,384]{1,0:T(8,128)S(1)}, f32[96,384]{1,0:T(8,128)}, u32[]{:S(2)}) copy-start(f32[96,384]{1,0:T(8,128)} %param.13) | copy-start | bytes 442372
  107.4 227.2 %reduce-scatter.9.cloned.1.call-start = ((), (), s32[]{:S(2)}) async-start(), calls=%async_computation.5 | async-start | bytes 1671168
  231.1 104.4 %copy-start.5 = (f32[96,384]{1,0:T(8,128)S(1)}, f32[96,384]{1,0:T(8,128)}, u32[]{:S(2)}) copy-start(f32[96,384]{1,0:T(8,128)} %param.14) | copy-start | bytes 442372
Sparse Core Ops, SparseCore 0:
  10.4 87.6 all-gather.1
  107.5 80.8 reduce-scatter.6
  231.3 103.2 reduce-scatter.8
